TPU v7x, 32 devices: a whole 2x2x4 slice. The times are simulated.
32 devices in a mesh: cin: 8 (over z, x), cout: 2 (over y), depth: 2 (over core).
Axes of the slice: x: 2, y: 2, z: 4, core: 2. Of those that a mesh axis runs over, the one named last changes fastest.
Arguments:
- features: bfloat16 [8, 512, 4, 128], P(None, 'cin', 'depth'), may hold values from -6 to 6
- kernel: bfloat16 [27, 512, 512], P(None, 'cout', 'cin'), may hold values from -0.0546875 to 0.0546875
- grad_out: bfloat16 [8, 512, 4, 128], P('cin', 'cout', 'depth'), may hold values from -6 to 6
Outputs:
- output: bfloat16 [8, 512, 4, 128], P('cin', 'cout', 'depth')
- input_grad: bfloat16 [8, 512, 4, 128], P('cout', 'cin', 'depth')
- kernel_grad: float32 [27, 512, 512], P(None, 'cout', 'cin')
All inputs are finite; a program needn't handle non-finite values.
Results may differ from a plain program's by a relative error of at most 0.001.
Values may be sent and summed in bfloat16 or wider, within the bound.
No kernel may reach another device: no remote copies, remote signals or barrier semaphores. Data moves between devices by JAX's collectives and lax.ppermute only.
A program may use at most 128 MiB of HBM per device.

v0:
```python
import math
import jax
import jax.numpy as jnp
from jax import lax
from jax.sharding import PartitionSpec as P


def padded_2(x, sides, width):
    for axis, dim in sides:
        size, length = (lax.axis_size(axis), x.shape[dim])
        up = [(i, (i + 1) % size) for i in range(size - 1)]
        down = [(j, i) for i, j in up]
        last = lax.slice_in_dim(x, length - width, length, axis=dim)
        first = lax.slice_in_dim(x, 0, width, axis=dim)
        before = lax.ppermute(last, axis, up)
        after = lax.ppermute(first, axis, down)
        x = jnp.concatenate([before, x, after], axis=dim)
    return x


def conv_rows(padded, weight, count, slab, width):
    total = None
    for depth_off in range(3):
        pieces = [
            padded[
                row_off : row_off + count,
                :,
                depth_off : depth_off + slab,
                col_off : col_off + width,
            ]
            for row_off in range(3)
            for col_off in range(3)
        ]
        stacked = jnp.stack(pieces, axis=1)
        term = jnp.einsum(
            "toc,htcdw->hodw",
            weight[9 * depth_off : 9 * depth_off + 9],
            stacked,
            preferred_element_type=jnp.float32,
        )
        total = term if total is None else total + term
    return total


def weight_terms(padded, grad_own, count, slab, width):
    parts = []
    for depth_off in range(3):
        pieces = [
            padded[
                row_off : row_off + count,
                :,
                depth_off : depth_off + slab,
                col_off : col_off + width,
            ]
            for row_off in range(3)
            for col_off in range(3)
        ]
        stacked = jnp.stack(pieces, axis=1)
        parts.append(
            jnp.einsum("hodw,htcdw->toc", grad_own, stacked, preferred_element_type=jnp.float32)
        )
    return jnp.concatenate(parts, axis=0)


def per_device(features, kernel, grad_out):
    rows_all = features.shape[0]
    slab = features.shape[2]
    width = features.shape[3]
    chan_in = features.shape[1]
    rows_own = rows_all // lax.axis_size("cin")
    slab_ext = padded_2(features, (("depth", 2),), 1)
    feat_pad = jnp.pad(slab_ext, ((1, 1), (0, 0), (0, 0), (1, 1)))
    block = feat_pad
    output = lax.psum_scatter(
        conv_rows(block, kernel, lax.axis_size("cin") * rows_own, slab, width),
        "cin",
        scatter_dimension=0,
        tiled=True,
    ).astype(jnp.bfloat16)
    grad_full = lax.all_gather(grad_out, "cin", axis=0, tiled=True)
    grad_full = padded_2(grad_full, (("depth", 2),), 1)
    grad_pad = jnp.pad(grad_full, ((1, 1), (0, 0), (0, 0), (0, 0)))
    rows_grad = rows_all // lax.axis_size("cout")
    block = grad_pad
    total = jnp.zeros((lax.axis_size("cout") * rows_grad, chan_in, slab, width), jnp.float32)
    for depth_off in range(3):
        part = block[:, :, 2 - depth_off : 2 - depth_off + slab, :]
        mixed = jnp.einsum(
            "toc,hodw->thcdw",
            kernel[9 * depth_off : 9 * depth_off + 9],
            part,
            preferred_element_type=jnp.float32,
        )
        mixed = jnp.pad(mixed, ((0, 0), (0, 0), (0, 0), (0, 0), (1, 1)))
        for row_off in range(3):
            for col_off in range(3):
                total = (
                    total
                    + mixed[
                        3 * row_off + col_off,
                        2 - row_off : 2 - row_off + lax.axis_size("cout") * rows_grad,
                        :,
                        :,
                        2 - col_off : 2 - col_off + width,
                    ]
                )
    input_grad = lax.psum_scatter(total, "cout", scatter_dimension=0, tiled=True).astype(
        jnp.bfloat16
    )
    grad_own = grad_full[:, :, 1 : 1 + slab, :]
    local_terms = weight_terms(feat_pad, grad_own, rows_all, slab, width)
    summed = lax.psum(local_terms, "depth")
    cells = rows_all * slab * lax.axis_size("depth") * width
    kernel_grad = summed * (1.0 / math.sqrt(cells))
    return (output, input_grad, kernel_grad)


def solution(mesh):
    return jax.shard_map(
        per_device,
        mesh=mesh,
        in_specs=(
            P(None, "cin", "depth", None),
            P(None, "cout", "cin"),
            P("cin", "cout", "depth", None),
        ),
        out_specs=(
            P("cin", "cout", "depth", None),
            P("cout", "cin", "depth", None),
            P(None, "cout", "cin"),
        ),
        check_vma=False,
    )
```

profile of v0, /device:TPU:0, one launch (start us, length us, event | category | flops | bytes accessed | tf_op | source)
XLA Modules:
  0.0 189.4 jit_solution(8112478354780090528)
XLA Ops:
  7.2 1.0 copy.40
  8.2 2.4 %collective-permute-start = (bf16[8,64,1,128]{3,1,2,0:T(8,128)(2,1)S(1)}, bf16[8,64,1,128]{3,1,2,0:T(8,128)(2,1)S(1)}, u32[]{:S(2)}, u32[]{:S(2)}) collective-permute-start(bf16[8,64,1,128]{3,1,2,0:T(8,128)(2,1)S(1)} %get-tuple-element.25), channel_id=1, source_target_pairs={{0,1},{2,3},{4,5},{6,7},{8,9},{10,11},{12,13},{14,15},{16,17},{18,... | collective-permute-start | bytes 393224 | tf_op jit(solution)/shard_map/ppermute | solution.py:15
  10.6 1.3 collective-permute-start.1
  11.9 1.6 copy.55
  19.3 1.0 fusion.83
  28.7 28.0 %all-gather.2.cloned.1.call-done = bf16[8,256,2,128]{3,1,2,0:T(8,128)(2,1)} async-done(((bf16[1,256,2,128]{3,1,2,0:T(8,128)(2,1)}), bf16[8,256,2,128]{3,1,2,0:T(8,128)(2,1)}) %all-gather.2.cloned.1.call-update) | async-done | bytes 1048592 | tf_op jit(solution)/shard_map/all_gather | solution.py:80
  56.7 1.4 fusion.104
  58.0 1.3 collective-permute-start.2
  59.4 1.3 collective-permute-start.3
  61.6 1.0 fusion.78
  66.5 0.9 convolution_bitcast_fusion
  67.4 3.3 %fusion.54 = f32[8,64,2,128]{3,1,2,0:T(8,128)} fusion(f32[9,10,64,2,128]{4,2,3,1,0:T(8,128)S(1)} %convolution_bitcast_fusion, f32[9,10,64,2,128]{4,2,3,1,0:T(8,128)S(1)} %convolution_bitcast_fusion.1, f32[9,10,64,2,128]{4,2,0,3,1:T(8,128)S(1)} %convolution_bitcast_fusion.2), kind=kLoop, calls=%fused_computation.90 | loop fusion | flops 3407872 | bytes 22937600 | tf_op jit(solution)/shard_map/add | solution.py:98
  70.8 2.5 %convolution_bitcast_fusion.3 = f32[9,256,64]{1,2,0:T(8,128)S(1)} fusion(bf16[8,9,64,2,128]{4,2,3,0,1:T(8,128)(2,1)} %fusion.68, bf16[8,256,2,128]{3,1,2,0:T(8,128)(2,1)S(1)} %copy-done), kind=kOutput, calls=%fused_computation.55 | convolution fusion | flops 603979776 | bytes 3997696 | tf_op jit(solution)/shard_map/hodw,htcdw->toc/dot_general | solution.py:60
  73.3 2.5 %convolution_bitcast_fusion.4 = f32[9,256,64]{1,2,0:T(8,128)S(1)} fusion(bf16[8,9,64,2,128]{4,2,3,0,1:T(8,128)(2,1)} %get-tuple-element.9, bf16[8,256,2,128]{3,1,2,0:T(8,128)(2,1)S(1)} %copy-done), kind=kOutput, calls=%fused_computation.56 | convolution fusion | flops 603979776 | bytes 3997696 | tf_op jit(solution)/shard_map/hodw,htcdw->toc/dot_general | solution.py:60
  75.8 2.6 %fusion.19 = f32[9,256,64]{1,2,0:T(8,128)S(1)} fusion(bf16[8,9,64,2,128]{4,2,1,3,0:T(8,128)(2,1)} %fusion.86, bf16[8,256,2,128]{3,1,2,0:T(8,128)(2,1)S(1)} %copy-done), kind=kOutput, calls=%fused_computation.54 | convolution fusion | flops 603979776 | bytes 3997696 | tf_op jit(solution)/shard_map/hodw,htcdw->toc/dot_general | solution.py:60
  78.3 1.4 pad_maximum_fusion
  80.0 2.7 %fusion.13 = f32[8,2,128,256,1]{3,2,0,1,4:T(8,128)S(1)} fusion(bf16[8,9,64,2,128]{4,2,3,0,1:T(8,128)(2,1)} %get-tuple-element.9, bf16[27,256,64]{1,2,0:T(8,128)(2,1)S(1)} %copy-done.1), kind=kOutput, calls=%fused_computation.40 | convolution fusion | flops 603979776 | bytes 4751360 | tf_op jit(solution)/shard_map/toc,htcdw->hodw/dot_general | solution.py:35
  82.7 2.7 %fusion.11 = f32[8,2,128,256,1]{3,2,0,1,4:T(8,128)S(1)} fusion(bf16[8,9,64,2,128]{4,2,3,0,1:T(8,128)(2,1)} %fusion.68, bf16[27,256,64]{1,2,0:T(8,128)(2,1)S(1)} %copy-done.1), kind=kOutput, calls=%fused_computation.38 | convolution fusion | flops 603979776 | bytes 4751360 | tf_op jit(solution)/shard_map/toc,htcdw->hodw/dot_general | solution.py:35
  85.5 4.1 %fusion.15 = f32[8,256,2,128]{1,3,2,0:T(8,128)} fusion(f32[8,2,128,256,1]{3,2,0,1,4:T(8,128)S(1)} %fusion.11, f32[8,2,128,256,1]{3,2,0,1,4:T(8,128)S(1)} %fusion.13, bf16[8,9,64,2,128]{4,2,1,3,0:T(8,128)(2,1)} %fusion.86, bf16[27,256,64]{1,2,0:T(8,128)(2,1)S(1)} %copy-done.1), kind=kOutput, calls=%fused_computation.43 | convolution fusion | flops 605028352 | bytes 8945664 | tf_op jit(solution)/shard_map/toc,htcdw->hodw/dot_general | solution.py:35
  89.6 1.0 convert_element_type.15
  91.4 17.4 %all-reduce.7.cloned.1.call-done = f32[27,256,64]{1,2,0:T(8,128)} async-done(((f32[27,256,64]{1,2,0:T(8,128)}), f32[27,256,64]{1,2,0:T(8,128)}) %all-reduce.7.cloned.1.call-update) | async-done | bytes 1769488 | tf_op jit(solution)/shard_map/psum | solution.py:112
  108.8 2.9 %broadcast_multiply_fusion = f32[27,256,64]{1,2,0:T(8,128)} fusion(f32[27,256,64]{1,2,0:T(8,128)} %all-reduce.7.cloned.1.call-done), kind=kLoop, calls=%fused_computation.58 | loop fusion | flops 442368 | bytes 3538944 | tf_op jit(solution)/shard_map/mul | solution.py:114
  111.7 69.4 %reduce-scatter.3.cloned.1.call-done = f32[1,256,2,128]{1,3,2,0:T(8,128)} async-done(((f32[8,256,2,128]{1,3,2,0:T(8,128)}), f32[1,256,2,128]{1,3,2,0:T(8,128)}) %reduce-scatter.3.cloned.1.call-update) | async-done | bytes 262160 | tf_op jit(solution)/shard_map/reduce_scatter | solution.py:74
  181.1 1.0 convert_element_type.14
  (44 shorter events, 20.9 us)
Async XLA Ops:
  7.2 49.5 %all-gather.2.cloned.1.call-start = ((), (), s32[]{:S(2)}) async-start(), calls=%async_computation.3 | async-start | bytes 1179648 | tf_op jit(solution)/shard_map/all_gather | solution.py:80
  8.2 5.3 %collective-permute-start = (bf16[8,64,1,128]{3,1,2,0:T(8,128)(2,1)S(1)}, bf16[8,64,1,128]{3,1,2,0:T(8,128)(2,1)S(1)}, u32[]{:S(2)}, u32[]{:S(2)}) collective-permute-start(bf16[8,64,1,128]{3,1,2,0:T(8,128)(2,1)S(1)} %get-tuple-element.25), channel_id=1, source_target_pairs={{0,1},{2,3},{4,5},{6,7},{8,9},{10,11},{12,13},{14,15},{16,17},{18,... | collective-permute-start | bytes 393224 | tf_op jit(solution)/shard_map/ppermute | solution.py:15
  10.6 3.2 %collective-permute-start.1 = (bf16[8,64,1,128]{3,1,2,0:T(8,128)(2,1)S(1)}, bf16[8,64,1,128]{3,1,2,0:T(8,128)(2,1)S(1)}, u32[]{:S(2)}, u32[]{:S(2)}) collective-permute-start(bf16[8,64,1,128]{3,1,2,0:T(8,128)(2,1)S(1)} %get-tuple-element.26), channel_id=1, source_target_pairs={{1,0},{3,2},{5,4},{7,6},{9,8},{11,10},{13,12},{15,14},{17,16},{19,... | collective-permute-start | bytes 393224 | tf_op jit(solution)/shard_map/ppermute | solution.py:16
  13.5 76.1 %reduce-scatter.5.cloned.1.call-start = ((), (), s32[]{:S(2)}) async-start(), calls=%async_computation.4 | async-start | bytes 786432 | tf_op jit(solution)/shard_map/reduce_scatter | solution.py:107
  16.8 5.2 %copy-start.2 = (bf16[8,64,2,128]{3,2,1,0:T(2,128)(2,1)S(1)}, bf16[8,64,2,128]{3,2,1,0:T(2,128)(2,1)}, u32[]{:S(2)}) copy-start(bf16[8,64,2,128]{3,2,1,0:T(2,128)(2,1)} %param.3) | copy-start | bytes 786436
  56.7 6.8 %copy-start = (bf16[8,256,2,128]{3,1,2,0:T(8,128)(2,1)S(1)}, bf16[8,256,2,128]{3,1,2,0:T(8,128)(2,1)}, u32[]{:S(2)}) copy-start(bf16[8,256,2,128]{3,1,2,0:T(8,128)(2,1)} %all-gather.2.cloned.1.call-done) | copy-start | bytes 3145732
  58.0 5.4 %collective-permute-start.2 = (bf16[8,256,1,128]{3,1,2,0:T(8,128)(2,1)S(1)}, bf16[8,256,1,128]{3,1,2,0:T(8,128)(2,1)S(1)}, u32[]{:S(2)}, u32[]{:S(2)}) collective-permute-start(bf16[8,256,1,128]{3,1,2,0:T(8,128)(2,1)S(1)} %get-tuple-element.23), channel_id=1, source_target_pairs={{0,1},{2,3},{4,5},{6,7},{8,9},{10,11},{12,13},{14,15},{16,17},{18,... | collective-permute-start | bytes 1572872 | tf_op jit(solution)/shard_map/ppermute | solution.py:15
  59.4 4.1 %collective-permute-start.3 = (bf16[8,256,1,128]{3,1,2,0:T(8,128)(2,1)S(1)}, bf16[8,256,1,128]{3,1,2,0:T(8,128)(2,1)S(1)}, u32[]{:S(2)}, u32[]{:S(2)}) collective-permute-start(bf16[8,256,1,128]{3,1,2,0:T(8,128)(2,1)S(1)} %get-tuple-element.24), channel_id=1, source_target_pairs={{1,0},{3,2},{5,4},{7,6},{9,8},{11,10},{13,12},{15,14},{17,16},{19,... | collective-permute-start | bytes 1572872 | tf_op jit(solution)/shard_map/ppermute | solution.py:16
  63.4 1.2 copy-start.1
  70.8 38.1 %all-reduce.7.cloned.1.call-start = ((), (), s32[]{:S(2)}) async-start(), calls=%async_computation.5 | async-start | bytes 3538944 | tf_op jit(solution)/shard_map/psum | solution.py:112
  79.7 101.4 %reduce-scatter.3.cloned.1.call-start = ((), (), s32[]{:S(2)}) async-start(), calls=%async_computation.2 | async-start | bytes 2359296 | tf_op jit(solution)/shard_map/reduce_scatter | solution.py:74
Sparse Core Ops, SparseCore 0:
  13.6 42.9 all-gather.1
  70.9 14.0 reduce-scatter.4
  88.1 20.6 all-reduce.6
  112.2 68.8 reduce-scatter.2
where the time goes:
time: 190 us; the launch traced here: 189 us
  waiting for transfers between devices  115 us (61%)
  local copies, waits for them, and re-layouts  21.9 us (12%)
  matrix products  19.9 us (10%)
  between operations  13.9 us (7%)
  other arithmetic  11.9 us (6%)
  starting transfers between devices  6.61 us (3%)
    reduce_scatter x1, waiting for transfers between devices, per_device(): lax.psum_scatter(conv_rows(block, kernel, lax.axis_size('cin') * rows_own...  69.4 us
    all_gather x1, waiting for transfers between devices, per_device(): grad_full = lax.all_gather(grad_out, 'cin', axis=0, tiled=True)  28 us
    unnamed x25, local copies, waits for them, and re-layouts  17.7 us
    psum x1, waiting for transfers between devices, per_device(): summed = lax.psum(local_terms, 'depth')  17.4 us
    dot_general x3, matrix products, conv_rows(): jnp.einsum('toc,htcdw->hodw', weight[9 * depth_off:9 * depth_off + 9], st...  9.56 us
    dot_general x3, matrix products, weight_terms(): jnp.einsum('hodw,htcdw->toc', grad_own, stacked, preferred_element_type=j...  7.5 us
  transfers between devices with their start and end apart: 8, of which 4 were waited for; matrix products, arithmetic and copies ran while one was open for 22% of the time, Pallas kernels for 0%

commit v1 on v0

--- a/solution.py
+++ b/solution.py
@@ -109,7 +109,7 @@
     )
     grad_own = grad_full[:, :, 1 : 1 + slab, :]
     local_terms = weight_terms(feat_pad, grad_own, rows_all, slab, width)
-    summed = lax.psum(local_terms, "depth")
+    summed = jnp.sum(lax.all_gather(local_terms, "depth"), axis=0)
     cells = rows_all * slab * lax.axis_size("depth") * width
     kernel_grad = summed * (1.0 / math.sqrt(cells))
     return (output, input_grad, kernel_grad)

time: 190 us -> 182 us (0.958)
  waiting for transfers between devices: 115 us -> 106 us
    psum x1 -> x0, waiting for transfers between devices: 17.4 us -> none  [per_device(): summed = lax.psum(local_terms, 'depth')]
    all_gather x0 -> x1, waiting for transfers between devices: none -> 12 us  [per_device(): summed = jnp.sum(lax.all_gather(local_terms, 'depth'), axis=0)]
    reduce_scatter x1, waiting for transfers between devices: 69.4 us -> 66.3 us  [per_device(): lax.psum_scatter(conv_rows(block, kernel, lax.axis_size('cin') * rows_own...]
    reduce_sum x0 -> x1, other arithmetic: none -> 2.46 us  [per_device(): summed = jnp.sum(lax.all_gather(local_terms, 'depth'), axis=0)]
    unnamed x25 -> x27, local copies, waits for them, and re-layouts: 17.7 us -> 17.7 us
  transfers between devices with their start and end apart: 8 -> 8, of which waited for: 4 -> 4; matrix products, arithmetic and copies ran while one was open for 22% -> 23% of each run, Pallas kernels for 0% -> 0%
where the time goes in v1:
time: 182 us
  waiting for transfers between devices  106 us (58%)
  local copies, waits for them, and re-layouts  21.8 us (12%)
  matrix products  20.2 us (11%)
  between operations  14 us (8%)
  other arithmetic  12.8 us (7%)
  starting transfers between devices  6.61 us (4%)
    reduce_scatter x1, waiting for transfers between devices, per_device(): lax.psum_scatter(conv_rows(block, kernel, lax.axis_size('cin') * rows_own...  66.3 us
    all_gather x1, waiting for transfers between devices, per_device(): grad_full = lax.all_gather(grad_out, 'cin', axis=0, tiled=True)  27.8 us
    unnamed x27, local copies, waits for them, and re-layouts  17.7 us
    all_gather x1, waiting for transfers between devices, per_device(): summed = jnp.sum(lax.all_gather(local_terms, 'depth'), axis=0)  12 us
    dot_general x3, matrix products, conv_rows(): jnp.einsum('toc,htcdw->hodw', weight[9 * depth_off:9 * depth_off + 9], st...  9.92 us
    dot_general x3, matrix products, weight_terms(): jnp.einsum('hodw,htcdw->toc', grad_own, stacked, preferred_element_type=j...  7.44 us
    ppermute x2, starting transfers between devices, padded_2(): before = lax.ppermute(last, axis, up)  3.69 us
  transfers between devices with their start and end apart: 8, of which 4 were waited for; matrix products, arithmetic and copies ran while one was open for 23% of the time, Pallas kernels for 0%

profile of v1, /device:TPU:0, one launch (start us, length us, event | category | flops | bytes accessed | tf_op | source)
XLA Modules:
  0.0 181.9 jit_solution(4241469650819792061)
XLA Ops:
  7.2 1.0 copy.40
  8.2 2.4 %collective-permute-start = (bf16[8,64,1,128]{3,1,2,0:T(8,128)(2,1)S(1)}, bf16[8,64,1,128]{3,1,2,0:T(8,128)(2,1)S(1)}, u32[]{:S(2)}, u32[]{:S(2)}) collective-permute-start(bf16[8,64,1,128]{3,1,2,0:T(8,128)(2,1)S(1)} %get-tuple-element.25), channel_id=1, source_target_pairs={{0,1},{2,3},{4,5},{6,7},{8,9},{10,11},{12,13},{14,15},{16,17},{18,... | collective-permute-start | bytes 393224 | tf_op jit(solution)/shard_map/ppermute | solution.py:15
  10.6 1.3 collective-permute-start.1
  11.9 1.6 copy.55
  19.3 1.0 fusion.83
  27.8 1.1 fusion.78
  28.9 27.8 %all-gather.4.cloned.1.call-done = bf16[8,256,2,128]{3,1,2,0:T(8,128)(2,1)} async-done(((bf16[1,256,2,128]{3,1,2,0:T(8,128)(2,1)}), bf16[8,256,2,128]{3,1,2,0:T(8,128)(2,1)}) %all-gather.4.cloned.1.call-update) | async-done | bytes 1048592 | tf_op jit(solution)/shard_map/all_gather | solution.py:80
  56.7 1.3 fusion.104
  58.0 1.3 collective-permute-start.2
  59.3 1.3 collective-permute-start.3
  61.5 2.8 %fusion.13 = f32[8,2,128,256,1]{3,2,0,1,4:T(8,128)S(1)} fusion(bf16[8,9,64,2,128]{4,2,3,0,1:T(8,128)(2,1)} %get-tuple-element.9, bf16[27,256,64]{1,2,0:T(8,128)(2,1)} %param.4), kind=kOutput, calls=%fused_computation.40 | convolution fusion | flops 603979776 | bytes 4751360 | tf_op jit(solution)/shard_map/toc,htcdw->hodw/dot_general | solution.py:35
  68.3 3.3 %fusion.54 = f32[8,64,2,128]{3,1,2,0:T(8,128)} fusion(f32[9,10,64,2,128]{4,2,3,1,0:T(8,128)S(1)} %convolution_bitcast_fusion, f32[9,10,64,2,128]{4,2,3,1,0:T(8,128)S(1)} %convolution_bitcast_fusion.1, f32[9,10,64,2,128]{4,2,0,3,1:T(8,128)S(1)} %convolution_bitcast_fusion.2), kind=kLoop, calls=%fused_computation.90 | loop fusion | flops 3407872 | bytes 22937600 | tf_op jit(solution)/shard_map/add | solution.py:98
  73.6 2.7 %fusion.11 = f32[8,2,128,256,1]{3,2,0,1,4:T(8,128)S(1)} fusion(bf16[8,9,64,2,128]{4,2,3,0,1:T(8,128)(2,1)} %fusion.68, bf16[27,256,64]{1,2,0:T(8,128)(2,1)} %param.4), kind=kOutput, calls=%fused_computation.38 | convolution fusion | flops 603979776 | bytes 4751360 | tf_op jit(solution)/shard_map/toc,htcdw->hodw/dot_general | solution.py:35
  76.3 4.4 %fusion.15 = f32[8,256,2,128]{1,3,2,0:T(8,128)} fusion(f32[8,2,128,256,1]{3,2,0,1,4:T(8,128)S(1)} %fusion.11, f32[8,2,128,256,1]{3,2,0,1,4:T(8,128)S(1)} %fusion.13, bf16[8,9,64,2,128]{4,2,1,3,0:T(8,128)(2,1)} %fusion.86, bf16[27,256,64]{1,2,0:T(8,128)(2,1)} %param.4), kind=kOutput, calls=%fused_computation.43 | convolution fusion | flops 605028352 | bytes 8945664 | tf_op jit(solution)/shard_map/toc,htcdw->hodw/dot_general | solution.py:35
  80.8 2.5 %convolution_bitcast_fusion.3 = f32[9,256,64]{1,2,0:T(8,128)S(1)} fusion(bf16[8,9,64,2,128]{4,2,3,0,1:T(8,128)(2,1)} %fusion.68, bf16[8,256,2,128]{3,1,2,0:T(8,128)(2,1)S(1)} %copy-done.1), kind=kOutput, calls=%fused_computation.55 | convolution fusion | flops 603979776 | bytes 3997696 | tf_op jit(solution)/shard_map/hodw,htcdw->toc/dot_general | solution.py:60
  83.3 2.5 %convolution_bitcast_fusion.4 = f32[9,256,64]{1,2,0:T(8,128)S(1)} fusion(bf16[8,9,64,2,128]{4,2,3,0,1:T(8,128)(2,1)} %get-tuple-element.9, bf16[8,256,2,128]{3,1,2,0:T(8,128)(2,1)S(1)} %copy-done.1), kind=kOutput, calls=%fused_computation.56 | convolution fusion | flops 603979776 | bytes 3997696 | tf_op jit(solution)/shard_map/hodw,htcdw->toc/dot_general | solution.py:60
  85.8 2.5 %fusion.19 = f32[9,256,64]{1,2,0:T(8,128)S(1)} fusion(bf16[8,9,64,2,128]{4,2,1,3,0:T(8,128)(2,1)} %fusion.86, bf16[8,256,2,128]{3,1,2,0:T(8,128)(2,1)S(1)} %copy-done.1), kind=kOutput, calls=%fused_computation.54 | convolution fusion | flops 603979776 | bytes 3997696 | tf_op jit(solution)/shard_map/hodw,htcdw->toc/dot_general | solution.py:60
  88.2 1.4 pad_maximum_fusion
  89.7 1.0 convert_element_type.15
  91.5 66.3 %reduce-scatter.3.cloned.1.call-done = f32[1,256,2,128]{1,3,2,0:T(8,128)} async-done(((f32[8,256,2,128]{1,3,2,0:T(8,128)}), f32[1,256,2,128]{1,3,2,0:T(8,128)}) %reduce-scatter.3.cloned.1.call-update) | async-done | bytes 262160 | tf_op jit(solution)/shard_map/reduce_scatter | solution.py:74
  157.7 1.0 convert_element_type.14
  159.5 12.0 %all-gather.6.cloned.1.call-done = f32[54,256,64]{1,2,0:T(8,128)} async-done(((f32[27,256,64]{1,2,0:T(8,128)}), f32[54,256,64]{1,2,0:T(8,128)}) %all-gather.6.cloned.1.call-update) | async-done | bytes 3538960 | tf_op jit(solution)/shard_map/all_gather | solution.py:112
  171.5 2.5 %reduce_sum.9 = f32[27,256,64]{1,2,0:T(8,128)S(1)} reduce(f32[2,27,256,64]{2,3,1,0:T(8,128)} %bitcast.378, f32[]{:T(128)} %constant.6.clone.1), dimensions={0}, to_apply=%region_2.3 | reduce | flops 442368 | bytes 5308420 | tf_op jit(solution)/shard_map/reduce_sum | solution.py:112
  174.0 1.4 broadcast_multiply_fusion
  (47 shorter events, 21.8 us)
Async XLA Ops:
  7.2 49.5 %all-gather.4.cloned.1.call-start = ((), (), s32[]{:S(2)}) async-start(), calls=%async_computation.3 | async-start | bytes 1179648 | tf_op jit(solution)/shard_map/all_gather | solution.py:80
  8.2 5.3 %collective-permute-start = (bf16[8,64,1,128]{3,1,2,0:T(8,128)(2,1)S(1)}, bf16[8,64,1,128]{3,1,2,0:T(8,128)(2,1)S(1)}, u32[]{:S(2)}, u32[]{:S(2)}) collective-permute-start(bf16[8,64,1,128]{3,1,2,0:T(8,128)(2,1)S(1)} %get-tuple-element.25), channel_id=1, source_target_pairs={{0,1},{2,3},{4,5},{6,7},{8,9},{10,11},{12,13},{14,15},{16,17},{18,... | collective-permute-start | bytes 393224 | tf_op jit(solution)/shard_map/ppermute | solution.py:15
  10.6 3.2 %collective-permute-start.1 = (bf16[8,64,1,128]{3,1,2,0:T(8,128)(2,1)S(1)}, bf16[8,64,1,128]{3,1,2,0:T(8,128)(2,1)S(1)}, u32[]{:S(2)}, u32[]{:S(2)}) collective-permute-start(bf16[8,64,1,128]{3,1,2,0:T(8,128)(2,1)S(1)} %get-tuple-element.26), channel_id=1, source_target_pairs={{1,0},{3,2},{5,4},{7,6},{9,8},{11,10},{13,12},{15,14},{17,16},{19,... | collective-permute-start | bytes 393224 | tf_op jit(solution)/shard_map/ppermute | solution.py:16
  13.5 76.2 %reduce-scatter.5.cloned.1.call-start = ((), (), s32[]{:S(2)}) async-start(), calls=%async_computation.4 | async-start | bytes 786432 | tf_op jit(solution)/shard_map/reduce_scatter | solution.py:107
  16.8 5.2 %copy-start.3 = (bf16[8,64,2,128]{3,2,1,0:T(2,128)(2,1)S(1)}, bf16[8,64,2,128]{3,2,1,0:T(2,128)(2,1)}, u32[]{:S(2)}) copy-start(bf16[8,64,2,128]{3,2,1,0:T(2,128)(2,1)} %param.3) | copy-start | bytes 786436
  58.0 6.3 %collective-permute-start.2 = (bf16[8,256,1,128]{3,1,2,0:T(8,128)(2,1)S(1)}, bf16[8,256,1,128]{3,1,2,0:T(8,128)(2,1)S(1)}, u32[]{:S(2)}, u32[]{:S(2)}) collective-permute-start(bf16[8,256,1,128]{3,1,2,0:T(8,128)(2,1)S(1)} %get-tuple-element.23), channel_id=1, source_target_pairs={{0,1},{2,3},{4,5},{6,7},{8,9},{10,11},{12,13},{14,15},{16,17},{18,... | collective-permute-start | bytes 1572872 | tf_op jit(solution)/shard_map/ppermute | solution.py:15
  59.3 5.0 %collective-permute-start.3 = (bf16[8,256,1,128]{3,1,2,0:T(8,128)(2,1)S(1)}, bf16[8,256,1,128]{3,1,2,0:T(8,128)(2,1)S(1)}, u32[]{:S(2)}, u32[]{:S(2)}) collective-permute-start(bf16[8,256,1,128]{3,1,2,0:T(8,128)(2,1)S(1)} %get-tuple-element.24), channel_id=1, source_target_pairs={{1,0},{3,2},{5,4},{7,6},{9,8},{11,10},{13,12},{15,14},{17,16},{19,... | collective-permute-start | bytes 1572872 | tf_op jit(solution)/shard_map/ppermute | solution.py:16
  61.5 2.8 %copy-start = (bf16[8,256,2,128]{3,1,2,0:T(8,128)(2,1)S(1)}, bf16[8,256,2,128]{3,1,2,0:T(8,128)(2,1)}, u32[]{:S(2)}) copy-start(bf16[8,256,2,128]{3,1,2,0:T(8,128)(2,1)} %all-gather.4.cloned.1.call-done) | copy-start | bytes 3145732
  64.3 1.2 copy-start.2
  71.6 86.1 %reduce-scatter.3.cloned.1.call-start = ((), (), s32[]{:S(2)}) async-start(), calls=%async_computation.2 | async-start | bytes 2359296 | tf_op jit(solution)/shard_map/reduce_scatter | solution.py:74
  76.3 4.5 %copy-start.1 = (bf16[8,256,2,128]{3,1,2,0:T(8,128)(2,1)S(1)}, bf16[8,256,2,128]{3,1,2,0:T(8,128)(2,1)}, u32[]{:S(2)}) copy-start(bf16[8,256,2,128]{3,1,2,0:T(8,128)(2,1)} %all-gather.4.cloned.1.call-done) | copy-start | bytes 3145732
  80.7 90.8 %all-gather.6.cloned.1.call-start = ((), (), s32[]{:S(2)}) async-start(), calls=%async_computation.5 | async-start | bytes 5308416 | tf_op jit(solution)/shard_map/all_gather | solution.py:112
Sparse Core Ops, SparseCore 0:
  13.6 42.9 all-gather.3
  71.7 14.0 reduce-scatter.4
  89.8 67.8 reduce-scatter.2
  159.8 11.6 all-gather.5
